TPU v7x, 32 devices: a whole 2x2x4 slice. The times are simulated.
32 devices in a mesh: gy: 4 (over y, core), gx: 8 (over z, x).
Axes of the slice: x: 2, y: 2, z: 4, core: 2. Of those that a mesh axis runs over, the one named last changes fastest.
Arguments:
- concentration: float32 [32, 1024, 1024], P('gx', None, 'gy'), may hold values from -3 to 3
Outputs:
- increment: float32 [32, 1024, 1024], P('gx', None, 'gy')
All inputs are finite; a program needn't handle non-finite values.
Results may differ from a plain program's by a relative error of at most 0.0003.
Values sent between devices are 32-bit elements; how exact they have to be, the bound alone decides.
A program may use at most 64 MiB of HBM per device.

v0:
```python
import jax
import jax.numpy as jnp
from jax import lax
from jax.sharding import PartitionSpec as P

BLK = 32


STRENGTH = 16.0
STEP = 2.0
HIGH = lax.Precision.HIGHEST


def extended(block, sides, width):
    for axis, dim in sides:
        count = lax.axis_size(axis)
        forward = [(i, i + 1) for i in range(count - 1)]
        backward = [(target, source) for source, target in forward]
        low = lax.ppermute(
            lax.slice_in_dim(block, block.shape[dim] - width, None, axis=dim), axis, forward
        )
        high = lax.ppermute(lax.slice_in_dim(block, 0, width, axis=dim), axis, backward)
        block = jnp.concatenate([low, block, high], axis=dim)
    return block


def laplace_inner(padded):
    total = padded[2:, 1:-1, 1:-1] + padded[:-2, 1:-1, 1:-1]
    total = total + padded[1:-1, 2:, 1:-1] + padded[1:-1, :-2, 1:-1]
    total = total + padded[1:-1, 1:-1, 2:] + padded[1:-1, 1:-1, :-2]
    return total - 6.0 * padded[1:-1, 1:-1, 1:-1]


def pad_x(values):
    return jnp.pad(values, ((0, 0), (1, 1), (0, 0)))


def product(matrix_a, matrix_b):
    return jnp.dot(matrix_a, matrix_b, precision=HIGH)


def banded_matrix(length):
    position = jnp.arange(length)
    distance = jnp.abs(position[:, None] - position[None, :])
    banded = jnp.where(
        distance == 0, 6.0, jnp.where(distance == 1, -4.0, jnp.where(distance == 2, 1.0, 0.0))
    )
    return jnp.eye(length, dtype=jnp.float32) + STRENGTH * banded.astype(jnp.float32)


def inverse_spd(matrix):
    factor = jnp.linalg.cholesky(matrix)
    return jax.scipy.linalg.cho_solve((factor, True), jnp.eye(matrix.shape[0], dtype=jnp.float32))


def operators(span_cells, blocks):
    inside = span_cells - 2
    inv_inner = inverse_spd(banded_matrix(inside))
    left = jnp.zeros((inside, 2), jnp.float32)
    left = left.at[0, 0].set(STRENGTH).at[0, 1].set(-4.0 * STRENGTH).at[1, 1].set(STRENGTH)
    right = jnp.zeros((inside, 2), jnp.float32)
    right = (
        right.at[inside - 2, 0]
        .set(STRENGTH)
        .at[inside - 1, 0]
        .set(-4.0 * STRENGTH)
        .at[inside - 1, 1]
        .set(STRENGTH)
    )
    w_left = product(inv_inner, left)
    w_right = product(inv_inner, right)
    sep_self = jnp.array(
        [[1.0 + 6.0 * STRENGTH, -4.0 * STRENGTH], [-4.0 * STRENGTH, 1.0 + 6.0 * STRENGTH]],
        jnp.float32,
    )
    diag_end = sep_self - product(right.T, w_right)
    diag_mid = diag_end - product(left.T, w_left)
    couple = product(right.T, w_left)
    corner_one = jnp.zeros((blocks, blocks), jnp.float32).at[blocks - 1, blocks - 1].set(1.0)
    system = jnp.kron(jnp.eye(blocks, dtype=jnp.float32), diag_mid) + jnp.kron(
        corner_one, diag_end - diag_mid
    )
    system = system - jnp.kron(jnp.eye(blocks, k=-1, dtype=jnp.float32), couple)
    system = system - jnp.kron(jnp.eye(blocks, k=1, dtype=jnp.float32), couple.T)
    return (inv_inner, left, right, w_left, w_right, inverse_spd(system))


def solve_lines(values, span_cells):
    leading, length, trailing = values.shape
    blocks = length // span_cells
    inside = span_cells - 2
    inv_inner, left, right, w_left, w_right, reduced_inv = operators(span_cells, blocks)
    shaped = values.reshape(leading, blocks, span_cells, trailing)
    partial_value = jnp.einsum("ij,apjb->apib", inv_inner, shaped[:, :, :inside], precision=HIGH)
    own_part = shaped[:, :, inside:] - jnp.einsum(
        "ji,apjb->apib", right, partial_value, precision=HIGH
    )
    left_part = -jnp.einsum("ji,apjb->apib", left, partial_value, precision=HIGH)
    further = jnp.concatenate([left_part[:, 1:], jnp.zeros_like(left_part[:, :1])], axis=1)
    reduced = (own_part + further).reshape(leading, 2 * blocks, trailing)
    separators = jnp.einsum("qr,arb->aqb", reduced_inv, reduced, precision=HIGH).reshape(
        leading, blocks, 2, trailing
    )
    previous = jnp.concatenate([jnp.zeros_like(separators[:, :1]), separators[:, :-1]], axis=1)
    interior = partial_value - jnp.einsum("ij,apjb->apib", w_left, previous, precision=HIGH)
    interior = interior - jnp.einsum("ij,apjb->apib", w_right, separators, precision=HIGH)
    return jnp.concatenate([interior, separators], axis=2).reshape(leading, length, trailing)


def solve_y(values):
    planes, rows_x, span_cells = values.shape
    inside = span_cells - 2
    blocks = lax.axis_size("gy")
    rank = lax.axis_index("gy")
    inv_inner, left, right, w_left, w_right, reduced_inv = operators(span_cells, blocks)
    lines = values.reshape(planes * rows_x, span_cells)
    count_lines = planes * rows_x
    partial_value = jnp.dot(lines[:, :inside], inv_inner.T, precision=HIGH)
    own_part = lines[:, inside:].T - jnp.einsum("ji,lj->il", right, partial_value, precision=HIGH)
    left_part = -jnp.einsum("ji,lj->il", left, partial_value, precision=HIGH)
    own_all, left_all = (
        lax.all_gather(own_part, "gy", axis=0, tiled=True),
        lax.all_gather(left_part, "gy", axis=0, tiled=True),
    )
    reduced = own_all + jnp.concatenate(
        [left_all[2:], jnp.zeros((2, count_lines), jnp.float32)], axis=0
    )
    separators = product(reduced_inv, reduced)
    padded = jnp.concatenate([jnp.zeros((2, count_lines), jnp.float32), separators], axis=0)
    paired = lax.dynamic_slice_in_dim(padded, 2 * rank, 4, 0)
    previous = paired[:2]
    current = paired[2:]
    interior = partial_value - jnp.einsum("ij,jl->li", w_left, previous, precision=HIGH)
    interior = interior - jnp.einsum("ij,jl->li", w_right, current, precision=HIGH)
    return jnp.concatenate([interior, current.T], axis=1).reshape(planes, rows_x, span_cells)


def solve_pencil(pencil):
    solved = solve_lines(pencil.reshape(1, pencil.shape[0], -1), BLK)
    return solved.reshape(pencil.shape)


def body(concentration):
    first_cycle = pad_x(extended(concentration, (("gy", 2), ("gx", 0)), 1))
    potential = (
        concentration * concentration * concentration - concentration - laplace_inner(first_cycle)
    )
    second_cycle = pad_x(extended(potential, (("gy", 2), ("gx", 0)), 1))
    source = STEP * laplace_inner(second_cycle)
    after_x = solve_lines(source, BLK)
    after_y = solve_y(after_x)
    pencil = lax.all_to_all(after_y, "gx", split_axis=1, concat_axis=0, tiled=True)
    solved = solve_pencil(pencil)
    return lax.all_to_all(solved, "gx", split_axis=0, concat_axis=1, tiled=True)


def solution(mesh):
    return jax.shard_map(
        body,
        mesh=mesh,
        in_specs=(P("gx", None, "gy"),),
        out_specs=P("gx", None, "gy"),
        check_vma=False,
    )
```

profile of v0, /device:TPU:0, one launch (start us, length us, event | category | flops | bytes accessed | tf_op | source)
XLA Modules:
  0.0 539.6 jit_solution(17909509076718153401)
XLA Ops:
  22.9 11.7 %cholesky.132 = f32[128,128]{1,0:T(8,128)S(1)} custom-call(f32[128,128]{1,0:T(8,128)S(1)} %cholesky.267), custom_call_target="Cholesky" | custom-call | tf_op jit(solution)/shard_map/jit(cholesky)/cholesky | solution.py:52
  34.7 9.8 %custom-call.56 = f32[1,128,128]{1,2,0:T(8,128)S(1)} custom-call(f32[1,128,128]{2,1,0:T(8,128)S(1)} %get-tuple-element.268), custom_call_target="InvertDiagBlocksLowerTriangular" | custom-call | tf_op jit(solution)/shard_map/jit(cholesky)/cholesky | solution.py:52
  45.0 11.5 %cholesky.224 = f32[126,126]{1,0:T(8,128)S(1)} custom-call(f32[126,126]{1,0:T(8,128)S(1)} %convolution_subtract_fusion.5), custom_call_target="Cholesky" | custom-call | tf_op jit(solution)/shard_map/jit(cholesky)/cholesky | solution.py:52
  59.2 20.1 %custom-call.57 = f32[2,128,128]{1,2,0:T(8,128)S(1)} custom-call(f32[2,128,128]{2,1,0:T(8,128)S(1)} %pad_maximum_fusion.29), custom_call_target="InvertDiagBlocksLowerTriangular" | custom-call | tf_op jit(solution)/shard_map/jit(_cho_solve)/triangular_solve | solution.py:53
  84.0 5.4 copy.94
  89.4 5.8 %cholesky.115 = f32[64,64]{1,0:T(8,128)S(1)} custom-call(f32[64,64]{1,0:T(8,128)S(1)} %fusion.65), custom_call_target="Cholesky" | custom-call | tf_op jit(solution)/shard_map/jit(cholesky)/cholesky | solution.py:52
  100.2 4.9 collective-permute-start.3
  107.5 18.4 %collective-permute-done.2 = f32[1,1024,258]{1,2,0:T(8,128)S(1)} collective-permute-done((f32[1,1024,258]{1,2,0:T(8,128)}, f32[1,1024,258]{1,2,0:T(8,128)S(1)}, u32[]{:S(2)}, u32[]{:S(2)}) %collective-permute-start.2) | collective-permute-done | bytes 1056800 | tf_op jit(solution)/shard_map/ppermute | solution.py:22
  126.0 25.7 %collective-permute-done.3 = f32[1,1024,258]{1,2,0:T(8,128)S(1)} collective-permute-done((f32[1,1024,258]{1,2,0:T(8,128)}, f32[1,1024,258]{1,2,0:T(8,128)S(1)}, u32[]{:S(2)}, u32[]{:S(2)}) %collective-permute-start.3) | collective-permute-done | bytes 1056800 | tf_op jit(solution)/shard_map/ppermute | solution.py:19
  151.6 6.7 %select_maximum_fusion.4 = f32[6,1026,258]{1,2,0:T(8,128)S(1)} fusion(f32[1,1024,258]{1,2,0:T(8,128)S(1)} %collective-permute-done.2, f32[1,1024,258]{1,2,0:T(8,128)S(1)} %collective-permute-done.3, f32[4,1024,1]{1,2,0:T(1,128)S(1)} %copy.102, f32[4,1024,256]{1,2,0:T(8,128)} %copy.94, f32[4,1024,1]{1,2,0:T(1,128)S(1)} %copy.100), kind=kLoop, calls=%fused_computation.11 | loop fusion | flops 19058976 | bytes 12693600 | tf_op jit(solution)/shard_map/concatenate | solution.py:23
  171.5 5.0 collective-permute-start.7
  177.2 4.9 custom-call.55
  184.1 13.5 %collective-permute-done.6 = f32[1,1024,258]{1,2,0:T(8,128)S(1)} collective-permute-done((f32[1,1024,258]{1,2,0:T(8,128)}, f32[1,1024,258]{1,2,0:T(8,128)S(1)}, u32[]{:S(2)}, u32[]{:S(2)}) %collective-permute-start.6) | collective-permute-done | bytes 1056800 | tf_op jit(solution)/shard_map/ppermute | solution.py:22
  197.6 25.5 %collective-permute-done.7 = f32[1,1024,258]{1,2,0:T(8,128)S(1)} collective-permute-done((f32[1,1024,258]{1,2,0:T(8,128)}, f32[1,1024,258]{1,2,0:T(8,128)S(1)}, u32[]{:S(2)}, u32[]{:S(2)}) %collective-permute-start.7) | collective-permute-done | bytes 1056800 | tf_op jit(solution)/shard_map/ppermute | solution.py:19
  223.1 6.7 %select_maximum_fusion = f32[6,1026,258]{1,2,0:T(8,128)S(1)} fusion(f32[1,1024,258]{1,2,0:T(8,128)S(1)} %collective-permute-done.6, f32[1,1024,258]{1,2,0:T(8,128)S(1)} %collective-permute-done.7, f32[4,1024,1]{1,2,0:T(1,128)S(1)} %copy.111, f32[4,1024,256]{1,2,0:T(8,128)} %copy-done, f32[4,1024,1]{1,2,0:T(1,128)S(1)} %copy.110), kind=kLoop, calls=%fused_computation.7 | loop fusion | flops 19058976 | bytes 12693600 | tf_op jit(solution)/shard_map/concatenate | solution.py:23
  229.7 8.1 %fusion.14 = f32[4,1024,256]{1,2,0:T(8,128)} fusion(f32[4,1024,256]{1,2,0:T(8,128)S(1)} %copy-done.1, f32[4,1024,1]{1,2,0:T(1,128)S(1)} %copy.110, f32[4,1024,1]{1,2,0:T(1,128)S(1)} %copy.111, f32[6,1026,258]{1,2,0:T(8,128)S(1)} %select_maximum_fusion, f32[1,1024,258]{1,2,0:T(8,128)S(1)} %collective-permute-done.7, f32[1,1024,258]{1,2,0:T(8,128)S(1)} %collective-permute-done.6), kind=kLoop, calls=%fused_computation.33 | loop fusion | flops 16777216 | bytes 18923520 | tf_op jit(solution)/shard_map/mul | solution.py:149
  237.9 5.4 copy.114
  243.2 5.6 %fusion.10 = f32[4,32,256,30]{2,3,1,0:T(8,128)S(1)} fusion(f32[4,32,32,256]{3,2,1,0:T(8,128)} %bitcast.238, f32[30,30]{1,0:T(8,128)S(1)} %fusion.70), kind=kOutput, calls=%fused_computation.28 | convolution fusion | flops 353894400 | bytes 8130064 | tf_op jit(solution)/shard_map/ij,apjb->apib/dot_general | solution.py:94
  251.8 4.3 fusion.35
  265.5 5.4 %fusion.8 = f32[4096,254]{0,1:T(8,128)} fusion(f32[4096,256]{1,0:T(8,128)S(1)} %bitcast.236, f32[126,254]{1,0:T(8,128)S(1)} %fusion.57, f32[128,254]{1,0:T(8,128)S(1)} %fusion.56), kind=kOutput, calls=%fused_computation.26 | convolution fusion | flops 3171154944 | bytes 8613904 | tf_op jit(solution)/shard_map/dot_general | solution.py:118
  272.2 4.4 fusion.4
  278.7 5.4 %all-gather = f32[4,2,4096]{2,1,0:T(2,128)S(1)} all-gather(f32[1,2,4096]{2,1,0:T(2,128)S(1)} %fusion.5), channel_id=1, replica_groups=mesh['gy'=4,'gx'=8] {'gy'}, dimensions={0}, use_global_device_ids=true | all-gather | bytes 163840 | tf_op jit(solution)/shard_map/all_gather | solution.py:122
  284.2 5.4 %all-gather.1 = f32[4,2,4096]{2,1,0:T(2,128)S(1)} all-gather(f32[1,2,4096]{2,1,0:T(2,128)S(1)} %fusion.4), channel_id=1, replica_groups=mesh['gy'=4,'gx'=8] {'gy'}, dimensions={0}, use_global_device_ids=true | all-gather | bytes 163840 | tf_op jit(solution)/shard_map/all_gather | solution.py:123
  290.0 5.8 %convolution_subtract_fusion.1 = f32[4096,254]{0,1:T(8,128)S(1)} fusion(f32[4096,254]{0,1:T(8,128)} %fusion.8, f32[254,2]{0,1:T(2,128)S(1)} %fusion.44, s32[]{:T(128)S(6)} %select_n.92, f32[8,4096]{1,0:T(8,128)S(1)} %fusion.46), kind=kOutput, calls=%fused_computation.18 | convolution fusion | flops 26009600 | bytes 8456180 | tf_op jit(solution)/shard_map/ij,jl->li/dot_general | solution.py:133
  301.8 6.0 %reshape.732 = f32[4,1024,256]{1,0,2:T(4,128)} reshape(f32[4096,256]{0,1:T(8,128)} %pad_maximum_fusion.17) | data formatting | bytes 8388608 | tf_op jit(solution)/shard_map/reshape | solution.py:135
  307.8 6.4 %copy.130 = f32[4,1024,256]{2,0,1:T(4,128)} copy(f32[4,1024,256]{1,0,2:T(4,128)} %reshape.732) | data formatting | bytes 8388608 | tf_op jit(solution)/shard_map/reshape | solution.py:135
  314.2 5.7 %all-to-all-start = ((f32[4,1024,256]{2,0,1:T(4,128)}), f32[4,1024,256]{2,0,1:T(4,128)}, u32[]{:S(2)}, u32[]{:S(2)}) async-start(f32[4,1024,256]{2,0,1:T(4,128)} %copy.130), calls=%async_computation | async-start | bytes 8388608 | tf_op jit(solution)/shard_map/all_to_all | solution.py:152
  322.3 91.4 %all-to-all-done = f32[4,1024,256]{2,0,1:T(4,128)} async-done(((f32[4,1024,256]{2,0,1:T(4,128)}), f32[4,1024,256]{2,0,1:T(4,128)}, u32[]{:S(2)}, u32[]{:S(2)}) %all-to-all-start) | async-done | bytes 4194336 | tf_op jit(solution)/shard_map/all_to_all | solution.py:152
  413.7 4.9 copy.155
  418.6 4.9 reshape_reshape.8
  423.6 5.6 %fusion.7 = f32[32768,30]{0,1:T(8,128)S(1)} fusion(f32[30,30]{1,0:T(8,128)S(1)} %fusion.70, f32[1,1,32,32768]{3,2,1,0:T(8,128)} %reshape_reshape.8), kind=kOutput, calls=%fused_computation.25 | convolution fusion | flops 353894400 | bytes 8130064 | tf_op jit(solution)/shard_map/ij,apjb->apib/dot_general | solution.py:94
  440.2 96.8 %all_to_all.33 = f32[32,128,256]{2,1,0:T(8,128)S(1)} all-to-all(f32[32,128,256]{2,1,0:T(8,128)S(1)} %pad_maximum_fusion.18), channel_id=1, replica_groups=mesh['gy'=4,'gx'=8] {'gx'}, dimensions={0} | all-to-all | bytes 8388608 | tf_op jit(solution)/shard_map/all_to_all | solution.py:154
  (172 shorter events, 90.2 us)
Async XLA Ops:
  4.2 14.4 %copy-start.9 = (f32[30,2]{0,1:T(2,128)S(1)}, f32[30,2]{0,1:T(2,128)}, u32[]{:S(2)}) copy-start(f32[30,2]{0,1:T(2,128)} %constant.822.clone.1) | copy-start | bytes 724
  4.2 16.3 %copy-start.10 = (f32[30,2]{0,1:T(2,128)S(1)}, f32[30,2]{0,1:T(2,128)}, u32[]{:S(2)}) copy-start(f32[30,2]{0,1:T(2,128)} %constant.821.clone.1) | copy-start | bytes 724
  4.2 16.6 %copy-start.13 = (f32[2,2]{0,1:T(2,128)S(1)}, f32[2,2]{0,1:T(2,128)}, u32[]{:S(2)}) copy-start(f32[2,2]{0,1:T(2,128)} %constant.836.clone) | copy-start | bytes 52
  4.2 17.4 %copy-start.8 = (f32[32,32]{1,0:T(8,128)S(1)}, f32[32,32]{1,0:T(8,128)}, u32[]{:S(2)}) copy-start(f32[32,32]{1,0:T(8,128)} %constant.825.clone.1) | copy-start | bytes 12292
  6.4 89.0 %collective-permute-start = (f32[4,1024,1]{1,0,2:T(4,128)S(1)}, f32[4,1024,1]{1,0,2:T(4,128)S(1)}, u32[]{:S(2)}, u32[]{:S(2)}) collective-permute-start(f32[4,1024,1]{1,0,2:T(4,128)S(1)} %copy.148), channel_id=1, source_target_pairs={{0,8},{8,16},{16,24},{1,9},{9,17},{17,25},{2,10},{10,18},{18,26},{... | collective-permute-start | bytes 49160 | tf_op jit(solution)/shard_map/ppermute | solution.py:19
  9.4 71.6 %copy-start.7 = (f32[254,2]{0,1:T(2,128)S(1)}, f32[254,2]{0,1:T(2,128)}, u32[]{:S(2)}) copy-start(f32[254,2]{0,1:T(2,128)} %constant.832.clone.1) | copy-start | bytes 6100
  9.4 73.1 %copy-start.6 = (f32[254,2]{1,0:T(8,128)S(1)}, f32[254,2]{1,0:T(8,128)}, u32[]{:S(2)}) copy-start(f32[254,2]{1,0:T(8,128)} %constant.831.clone.1) | copy-start | bytes 6100
  9.4 86.1 %collective-permute-start.1 = (f32[4,1024,1]{1,0,2:T(4,128)S(1)}, f32[4,1024,1]{1,0,2:T(4,128)S(1)}, u32[]{:S(2)}, u32[]{:S(2)}) collective-permute-start(f32[4,1024,1]{1,0,2:T(4,128)S(1)} %copy.149), channel_id=1, source_target_pairs={{8,0},{16,8},{24,16},{9,1},{17,9},{25,17},{10,2},{18,10},{26,18},{... | collective-permute-start | bytes 49160 | tf_op jit(solution)/shard_map/ppermute | solution.py:22
  89.4 15.8 %copy-start.11 = (f32[4,4]{1,0:T(4,128)S(1)}, f32[4,4]{1,0:T(4,128)}, u32[]{:S(2)}) copy-start(f32[4,4]{1,0:T(4,128)} %constant.833.clone.1) | copy-start | bytes 196
  98.9 27.1 %collective-permute-start.2 = (f32[1,1024,258]{1,2,0:T(8,128)}, f32[1,1024,258]{1,2,0:T(8,128)S(1)}, u32[]{:S(2)}, u32[]{:S(2)}) collective-permute-start(f32[1,1024,258]{1,2,0:T(8,128)} %get-tuple-element.260), channel_id=1, source_target_pairs={{1,0},{2,1},{3,2},{4,3},{5,4},{6,5},{7,6},{9,8},{10,9},{11,10},{12... | collective-permute-start | bytes 3170312 | tf_op jit(solution)/shard_map/ppermute | solution.py:22
  100.2 51.5 %collective-permute-start.3 = (f32[1,1024,258]{1,2,0:T(8,128)}, f32[1,1024,258]{1,2,0:T(8,128)S(1)}, u32[]{:S(2)}, u32[]{:S(2)}) collective-permute-start(f32[1,1024,258]{1,2,0:T(8,128)} %get-tuple-element.259), channel_id=1, source_target_pairs={{0,1},{1,2},{2,3},{3,4},{4,5},{5,6},{6,7},{8,9},{9,10},{10,11},{11... | collective-permute-start | bytes 3170312 | tf_op jit(solution)/shard_map/ppermute | solution.py:19
  107.5 50.8 %copy-start.5 = (f32[4,1024,256]{1,2,0:T(8,128)S(1)}, f32[4,1024,256]{1,2,0:T(8,128)}, u32[]{:S(2)}) copy-start(f32[4,1024,256]{1,2,0:T(8,128)} %copy.94) | copy-start | bytes 12582916
  162.0 6.7 %copy-start = (f32[4,1024,256]{1,2,0:T(8,128)}, f32[4,1024,256]{1,2,0:T(8,128)S(1)}, u32[]{:S(2)}) copy-start(f32[4,1024,256]{1,2,0:T(8,128)S(1)} %fusion.6) | copy-start | bytes 12582916
  162.0 3.5 collective-permute-start.4
  164.2 4.4 collective-permute-start.5
  170.3 27.3 %collective-permute-start.6 = (f32[1,1024,258]{1,2,0:T(8,128)}, f32[1,1024,258]{1,2,0:T(8,128)S(1)}, u32[]{:S(2)}, u32[]{:S(2)}) collective-permute-start(f32[1,1024,258]{1,2,0:T(8,128)} %get-tuple-element.258), channel_id=1, source_target_pairs={{1,0},{2,1},{3,2},{4,3},{5,4},{6,5},{7,6},{9,8},{10,9},{11,10},{12... | collective-permute-start | bytes 3170312 | tf_op jit(solution)/shard_map/ppermute | solution.py:22
  171.5 51.5 %collective-permute-start.7 = (f32[1,1024,258]{1,2,0:T(8,128)}, f32[1,1024,258]{1,2,0:T(8,128)S(1)}, u32[]{:S(2)}, u32[]{:S(2)}) collective-permute-start(f32[1,1024,258]{1,2,0:T(8,128)} %get-tuple-element.257), channel_id=1, source_target_pairs={{0,1},{1,2},{2,3},{3,4},{4,5},{5,6},{6,7},{8,9},{9,10},{10,11},{11... | collective-permute-start | bytes 3170312 | tf_op jit(solution)/shard_map/ppermute | solution.py:19
  184.1 45.6 %copy-start.1 = (f32[4,1024,256]{1,2,0:T(8,128)S(1)}, f32[4,1024,256]{1,2,0:T(8,128)}, u32[]{:S(2)}) copy-start(f32[4,1024,256]{1,2,0:T(8,128)} %copy-done) | copy-start | bytes 12582916
  248.8 2.9 copy-start.3
  248.9 2.9 copy-start.12
  256.9 3.5 copy-start.4
  272.2 4.4 copy-start.2
  314.2 99.5 %all-to-all-start = ((f32[4,1024,256]{2,0,1:T(4,128)}), f32[4,1024,256]{2,0,1:T(4,128)}, u32[]{:S(2)}, u32[]{:S(2)}) async-start(f32[4,1024,256]{2,0,1:T(4,128)} %copy.130), calls=%async_computation | async-start | bytes 8388608 | tf_op jit(solution)/shard_map/all_to_all | solution.py:152
where the time goes:
time: 549 us; the launch traced here: 540 us
  waiting for transfers between devices  178 us (32%)
  other arithmetic  113 us (21%)
  blocking collectives  108 us (20%)
  matrix products  62.5 us (11%)
  local copies, waits for them, and re-layouts  51.8 us (9%)
  starting transfers between devices  25.4 us (5%)
    all_to_all x1, blocking collectives, body(): return lax.all_to_all(solved, 'gx', split_axis=0, concat_axis=1, tiled=True)  96.8 us
    all_to_all x1, waiting for transfers between devices, body(): lax.all_to_all(after_y, 'gx', split_axis=1, concat_axis=0, tiled=True)  91.4 us
    ppermute x4, waiting for transfers between devices, extended(): lax.ppermute(lax.slice_in_dim(block, block.shape[dim] - width, None, axis...  51.1 us
    another operation x19, other arithmetic, inverse_spd(): factor = jnp.linalg.cholesky(matrix)  46.8 us
    ppermute x4, waiting for transfers between devices, extended(): lax.ppermute(lax.slice_in_dim(block, 0, width, axis=dim), axis, backward)  35 us
    another operation x14, other arithmetic, inverse_spd(): jax.scipy.linalg.cho_solve((factor, True), jnp.eye(matrix.shape[0], dtype...  30.8 us
    concatenate x4, other arithmetic, extended(): block = jnp.concatenate([low, block, high], axis=dim)  18.3 us
    ppermute x4, starting transfers between devices, extended(): lax.ppermute(lax.slice_in_dim(block, block.shape[dim] - width, None, axis...  14.4 us
  transfers between devices with their start and end apart: 9, of which 6 were waited for; matrix products, arithmetic and copies ran while one was open for 18% of the time, Pallas kernels for 0%

commit v1 on v0

v1 whole, which is shorter than its diff:
```python
import functools

import jax
import jax.numpy as jnp
import numpy as np
from jax import lax
from jax.experimental import pallas as pl
from jax.experimental.pallas import tpu as pltpu
from jax.sharding import PartitionSpec as P

STRENGTH = 16.0
STEP = 2.0
HALO = 2
CHUNKS = 2
FINE = lax.Precision.HIGHEST


def banded(length):
    eye = functools.partial(np.eye, length)
    stencil = 6.0 * eye() - 4.0 * (eye(k=1) + eye(k=-1)) + eye(k=2) + eye(k=-2)
    return eye() + STRENGTH * stencil


def coupling():
    return STRENGTH * np.array([[1.0, 0.0], [-4.0, 1.0]])


def split_line_maps(length, blocks):
    span = length // blocks
    local = np.linalg.inv(banded(span))
    cross = coupling()
    rows = np.array([0, 1, span - 2, span - 1])
    feed = np.zeros((blocks, span, 4 * blocks))
    for block in range(blocks):
        if block > 0:
            feed[block][:, 4 * block - 2 : 4 * block] = local[:, :2] @ cross.T
        if block < blocks - 1:
            feed[block][:, 4 * block + 4 : 4 * block + 6] = local[:, -2:] @ cross
    system = np.eye(4 * blocks) + np.concatenate([feed[b][rows] for b in range(blocks)])
    correct = feed @ np.linalg.inv(system)
    as32 = lambda a: np.ascontiguousarray(a, dtype=np.float32)
    return as32(local), as32(local[rows]), as32(correct)


def two_ended_maps(length, groups):
    span = length // groups
    half = groups // 2
    cross = coupling()
    inner = np.zeros((span, 2))
    inner[-2:] = cross
    outer = np.zeros((span, 2))
    outer[:2] = cross.T
    edge_maps, full_maps = [], []
    corner = np.zeros((2, 2))
    inverses = []
    for depth in range(half):
        schur = banded(span)
        schur[:2, :2] -= cross.T @ corner @ cross
        inverse = np.linalg.inv(schur)
        inverses.append(inverse)
        corner = inverse[-2:, -2:]
        reach = outer if depth > 0 else np.zeros_like(outer)
        edge_maps.append(np.concatenate([inverse, -inverse @ reach], axis=1))
    for depth in range(half):
        known = edge_maps[depth]
        back = inverses[depth] @ inner
        if depth < half - 1:
            full_maps.append(np.concatenate([known, -back], axis=1))
        else:
            swap = np.eye(2)[::-1]
            hold = back[-2:]
            far = swap @ hold @ swap
            joint = np.linalg.inv(np.eye(2) - far @ hold)
            own = known - back @ joint @ (-far) @ known[-2:]
            full_maps.append(np.concatenate([own, -back @ joint], axis=1))
    flip = np.arange(span)[::-1]
    two = np.array([1, 0])
    edges, outs, fulls = [], [], []
    for group in range(groups):
        mirrored = group >= half
        depth = groups - 1 - group if mirrored else group
        edge, full = edge_maps[depth][-2:], full_maps[depth]
        if mirrored:
            columns = np.concatenate([flip, span + two, span + 2 + two])
            edge = edge[two][:, columns[: span + 2]]
            full = full[flip][:, columns]
            out = full[-2:]
        else:
            out = full[:2]
        edges.append(edge)
        outs.append(out)
        fulls.append(full)
    stack = lambda a: np.ascontiguousarray(np.stack(a), dtype=np.float32)
    return stack(edges), stack(outs), stack(fulls)


def mix_kernel(counts, matrix_ref, *refs):
    out_ref = refs[-1]
    inputs = refs[:-1]
    for row in range(out_ref.shape[0]):
        total, column = None, 0
        for ref, count in zip(inputs, counts):
            for plane in range(count):
                term = matrix_ref[row, column] * ref[plane]
                total = term if total is None else total + term
                column += 1
        out_ref[row] = total


def mix(matrix, *arrays):
    counts = tuple(a.shape[0] for a in arrays)
    rows, width = arrays[0].shape[1:]
    tile = 32
    spec = lambda planes: pl.BlockSpec((planes, tile, width), lambda i: (0, i, 0))
    total = sum(counts) + matrix.shape[0]
    return pl.pallas_call(
        functools.partial(mix_kernel, counts),
        grid=(rows // tile,),
        in_specs=[pl.BlockSpec(memory_space=pltpu.SMEM)] + [spec(c) for c in counts],
        out_specs=spec(matrix.shape[0]),
        out_shape=jax.ShapeDtypeStruct((matrix.shape[0], rows, width), jnp.float32),
        cost_estimate=pl.CostEstimate(
            flops=2 * matrix.shape[0] * sum(counts) * rows * width,
            bytes_accessed=4 * total * rows * width,
            transcendentals=0,
        ),
    )(matrix, *arrays)


def laplace_inner(padded):
    total = padded[2:, 1:-1, 1:-1] + padded[:-2, 1:-1, 1:-1]
    total = total + padded[1:-1, 2:, 1:-1] + padded[1:-1, :-2, 1:-1]
    total = total + padded[1:-1, 1:-1, 2:] + padded[1:-1, 1:-1, :-2]
    return total - 6.0 * padded[1:-1, 1:-1, 1:-1]


def pick(table, index):
    return lax.dynamic_index_in_dim(jnp.asarray(table), index, 0, keepdims=False)


def pad_x(values):
    return jnp.pad(values, ((0, 0), (1, 1), (0, 0)))


def body(concentration):
    planes, cells_x, cells_y = concentration.shape
    count, blocks = lax.axis_size("gx"), lax.axis_size("gy")
    groups, half_x = count // 2, cells_x // 2
    rank, rank_y = lax.axis_index("gx"), lax.axis_index("gy")
    side, group = rank % 2, rank // 2
    first = side == 0
    rows = half_x + 8
    partner = [(i, i ^ 1) for i in range(count)]
    up = [(i, i + 2) for i in range(count - 2)]
    down = [(b, a) for a, b in up]

    own = lax.dynamic_slice_in_dim(concentration, side * (cells_x - rows), rows, 1)
    give = lax.dynamic_slice_in_dim(concentration, (1 - side) * (cells_x - rows), rows, 1)
    got = lax.ppermute(give, "gx", partner)
    low, high = jnp.where(first, own, got), jnp.where(first, got, own)
    below = lax.ppermute(high[-HALO:], "gx", up)
    above = lax.ppermute(low[:HALO], "gx", down)
    block = jnp.concatenate([below, low, high, above], axis=0)
    right = [(i, i + 1) for i in range(blocks - 1)]
    left = [(b, a) for a, b in right]
    columns = lambda v: jnp.moveaxis(v, 2, 0)
    before = lax.ppermute(columns(block[:, :, -HALO:]), "gy", right)
    behind = lax.ppermute(columns(block[:, :, :HALO]), "gy", left)
    wide = jnp.concatenate(
        [jnp.moveaxis(before, 0, 2), block, jnp.moveaxis(behind, 0, 2)], axis=2
    )
    centre = wide[1:-1, :, 1:-1]
    potential = centre * centre * centre - centre - laplace_inner(pad_x(wide))
    layer = lax.broadcasted_iota(jnp.int32, potential.shape, 0)
    column = lax.broadcasted_iota(jnp.int32, potential.shape, 2)
    outside = (layer == 0) & (group == 0)
    outside |= (layer == potential.shape[0] - 1) & (group == groups - 1)
    outside |= (column == 0) & (rank_y == 0)
    outside |= (column == cells_y + 1) & (rank_y == blocks - 1)
    potential = jnp.where(outside, 0.0, potential)
    source = STEP * laplace_inner(pad_x(potential))
    source = lax.dynamic_slice_in_dim(source, side * 8, half_x, 1)

    edge_map, out_map, full_map = two_ended_maps(planes * count, groups)
    edge_map, out_map, full_map = (pick(t, group) for t in (edge_map, out_map, full_map))
    middle = groups // 2
    def hop(values, sends):
        return lax.ppermute(
            values, "gx", [(2 * a + s, 2 * b + s) for a, b in sends for s in range(2)]
        )
    inward = [
        [(d, d + 1), (groups - 1 - d, groups - 2 - d)] for d in range(middle - 1)
    ]
    chunk = half_x // CHUNKS
    pieces = []
    for part in range(CHUNKS):
        piece = source[:, part * chunk : (part + 1) * chunk]
        outer = jnp.zeros((2, chunk, cells_y), jnp.float32)
        for step, sends in enumerate(inward):
            if step == 0:
                edge = mix(edge_map[:, : 2 * planes], piece)
                outer = hop(edge, sends)
            else:
                outer = outer + hop(mix(edge_map, piece, outer), sends)
        inner = hop(
            mix(edge_map, piece, outer), [(middle - 1, middle), (middle, middle - 1)]
        )
        for sends in reversed(inward):
            inner = inner + hop(mix(out_map, piece, outer, inner), [(b, a) for a, b in sends])
        solved = mix(full_map, piece, outer, inner)
        keep = jnp.where(first, solved[:planes], solved[planes:])
        send = jnp.where(first, solved[planes:], solved[:planes])
        back = lax.ppermute(send, "gx", partner)
        pieces.append((jnp.where(first, keep, back), jnp.where(first, back, keep)))
    after_z = jnp.concatenate([p[0] for p in pieces] + [p[1] for p in pieces], axis=1)

    local, edge_rows, correct = split_line_maps(cells_y * blocks, blocks)
    edges = jnp.einsum("ij,axj->iax", edge_rows, after_z, precision=FINE)
    edges = edges.reshape(4, planes * cells_x)
    everyone = lax.all_gather(edges, "gy", axis=0, tiled=True)
    everyone = everyone.reshape(4 * blocks, planes, cells_x)
    after_y = jnp.einsum("axj,ji->axi", after_z, local, precision=FINE)
    after_y = after_y - jnp.einsum("qax,iq->axi", everyone, pick(correct, rank_y), precision=FINE)

    inverse_x = np.ascontiguousarray(np.linalg.inv(banded(cells_x)), dtype=np.float32)
    return jnp.einsum("ij,ajb->aib", inverse_x, after_y, precision=FINE)


def solution(mesh):
    return jax.shard_map(
        body,
        mesh=mesh,
        in_specs=(P("gx", None, "gy"),),
        out_specs=P("gx", None, "gy"),
        check_vma=False,
    )
```

time: 549 us -> 327 us (0.60); the launches traced: 540 us -> 326 us
  blocking collectives: 108 us -> 6.54 us
  waiting for transfers between devices: 178 us -> 121 us
  other arithmetic: 113 us -> 63.8 us
  Pallas kernels: 0 us -> 45.9 us
  matrix products: 62.5 us -> 30.2 us
  local copies, waits for them, and re-layouts: 51.8 us -> 35.4 us
    all_to_all x1 -> x0, blocking collectives: 96.8 us -> none  [body(): return lax.all_to_all(solved, 'gx', split_axis=0, concat_axis=1, tiled=True)]
    all_to_all x1 -> x0, waiting for transfers between devices: 91.4 us -> none  [body(): lax.all_to_all(after_y, 'gx', split_axis=1, concat_axis=0, tiled=True)]
    another operation x33 -> x0, other arithmetic: 77.5 us -> none  [the longest x19 46.8 us: inverse_spd(): factor = jnp.linalg.cholesky(matrix)]
    pallas_call x0 -> x8, Pallas kernels: none -> 45.9 us  [mix(): pl.pallas_call(functools.partial(mix_kernel, counts), grid=(rows // tile,...]
    ppermute x8 -> x13, waiting for transfers between devices: 86.1 us -> 121 us  [the longest x1 46.4 us: body(): got = lax.ppermute(give, 'gx', partner)]
    dot_general x26 -> x4, matrix products: 59 us -> 30.2 us  [the longest x1 15.1 us: body(): return jnp.einsum('ij,ajb->aib', inverse_x, after_y, precision=FINE)]
    select_n x0 -> x6, other arithmetic: none -> 27.1 us  [the longest x1 17.2 us: body(): potential = jnp.where(outside, 0.0, potential)]
    add x5 -> x3, other arithmetic: 0.03 us -> 14.3 us  [the longest x1 11.5 us: laplace_inner(): total = padded[2:, 1:-1, 1:-1] + padded[:-2, 1:-1, 1:-1]]
  transfers between devices with their start and end apart: 9 -> 13, of which waited for: 6 -> 10; matrix products, arithmetic and copies ran while one was open for 18% -> 6% of each run, Pallas kernels for 0% -> 12%
where the time goes in v1:
time: 327 us; the launch traced here: 326 us
  waiting for transfers between devices  121 us (37%)
  other arithmetic  63.8 us (20%)
  Pallas kernels  45.9 us (14%)
  local copies, waits for them, and re-layouts  35.4 us (11%)
  matrix products  30.2 us (9%)
  starting transfers between devices  22.8 us (7%)
  blocking collectives  6.54 us (2%)
    ppermute x1, waiting for transfers between devices, body(): got = lax.ppermute(give, 'gx', partner)  46.4 us
    pallas_call x8, Pallas kernels, mix(): pl.pallas_call(functools.partial(mix_kernel, counts), grid=(rows // tile,...  45.9 us
    ppermute x2, waiting for transfers between devices, body(): back = lax.ppermute(send, 'gx', partner)  33.1 us
    ppermute x1, waiting for transfers between devices, body(): below = lax.ppermute(high[-HALO:], 'gx', up)  18.5 us
    select_n x1, other arithmetic, body(): potential = jnp.where(outside, 0.0, potential)  17.2 us
    ppermute x6, waiting for transfers between devices, hop(): lax.ppermute(values, 'gx', [(2 * a + s, 2 * b + s) for a, b in sends for...  16.2 us
    dot_general x1, matrix products, body(): return jnp.einsum('ij,ajb->aib', inverse_x, after_y, precision=FINE)  15.1 us
    mul x1, other arithmetic, body(): source = STEP * laplace_inner(pad_x(potential))  11.9 us
  transfers between devices with their start and end apart: 13, of which 10 were waited for; matrix products, arithmetic and copies ran while one was open for 6% of the time, Pallas kernels for 12%

profile of v1, /device:TPU:0, one launch (start us, length us, event | category | flops | bytes accessed | tf_op | source)
XLA Modules:
  0.0 325.5 jit_solution(16184401734342867779)
XLA Ops:
  1.7 3.0 collective-permute-start
  4.7 46.4 %collective-permute-done = f32[4,520,256]{2,1,0:T(8,128)} collective-permute-done((f32[4,520,256]{2,1,0:T(8,128)S(1)}, f32[4,520,256]{2,1,0:T(8,128)}, u32[]{:S(2)}, u32[]{:S(2)}) %collective-permute-start) | collective-permute-done | bytes 2129952 | tf_op jit(solution)/shard_map/ppermute | solution.py:159
  51.2 2.7 dynamic-slice_select_fusion.1
  55.1 3.8 %collective-permute-start.1 = (f32[2,520,256]{2,1,0:T(8,128)}, f32[2,520,256]{2,1,0:T(8,128)S(1)}, u32[]{:S(2)}, u32[]{:S(2)}) collective-permute-start(f32[2,520,256]{2,1,0:T(8,128)} %slice.118), channel_id=1, source_target_pairs={{0,2},{1,3},{2,4},{3,5},{4,6},{5,7},{8,10},{9,11},{10,12},{11,13},... | collective-permute-start | bytes 3194888 | tf_op jit(solution)/shard_map/ppermute | solution.py:161
  62.5 18.5 %collective-permute-done.1 = f32[2,520,256]{2,1,0:T(8,128)S(1)} collective-permute-done((f32[2,520,256]{2,1,0:T(8,128)}, f32[2,520,256]{2,1,0:T(8,128)S(1)}, u32[]{:S(2)}, u32[]{:S(2)}) %collective-permute-start.1) | collective-permute-done | bytes 1064992 | tf_op jit(solution)/shard_map/ppermute | solution.py:161
  81.0 5.2 %collective-permute-done.2 = f32[2,520,256]{2,1,0:T(8,128)} collective-permute-done((f32[2,520,256]{2,1,0:T(8,128)}, f32[2,520,256]{2,1,0:T(8,128)}, u32[]{:S(2)}, u32[]{:S(2)}) %collective-permute-start.2) | collective-permute-done | bytes 1064992 | tf_op jit(solution)/shard_map/ppermute | solution.py:162
  88.3 3.7 %slice_bitcast_fusion.1 = (f32[2,12,520]{0,2,1:T(8,128)}, f32[2,12,520]{0,2,1:T(8,128)}) fusion(f32[12,520,256]{2,1,0:T(8,128)S(1)} %pad_maximum_fusion.9), kind=kLoop, calls=%fused_computation.35 | loop fusion | bytes 199680 | tf_op jit(solution)/shard_map/transpose | solution.py:166
  105.6 8.3 %pad_maximum_fusion = f32[12,520,260]{2,1,0:T(8,128)S(1)} fusion(f32[12,520,2]{2,1,0:T(8,128)} %bitcast.28, f32[2,520,256]{2,1,0:T(8,128)} %collective-permute-done.2, f32[4,520,256]{2,1,0:T(8,128)S(1)} %get-tuple-element.13, f32[4,520,256]{2,1,0:T(8,128)} %copy-done.1, f32[2,520,256]{2,1,0:T(8,128)S(1)} %collective-permute-done.1, f32[12,520,2]{2,1,0:T(8,128)} %bitcast.26), kind=kLoop, calls=%fused_computation.1 | loop fusion | flops 8112000 | bytes 12979200 | tf_op jit(solution)/shard_map/concatenate | solution.py:169
  113.9 17.2 %fusion.6 = f32[10,520,258]{2,1,0:T(8,128)S(1)} fusion(f32[12,520,260]{2,1,0:T(8,128)S(1)} %pad_maximum_fusion, f32[12,520,2]{2,1,0:T(8,128)} %bitcast.27, f32[2,520,256]{2,1,0:T(8,128)} %collective-permute-done.2, f32[4,520,256]{2,1,0:T(8,128)} %copy-done, f32[4,520,256]{2,1,0:T(8,128)} %copy-done.1, f32[2,520,256]{2,1,0:T(8,128)S(1)} %collective-permute-done.1, ...), kind=kLoop, calls=%fused_computation.10 | loop fusion | flops 29515200 | bytes 45403776 | tf_op jit(solution)/shard_map/jit(_where)/select_n | solution.py:180
  131.1 11.5 %slice_add_fusion.1 = (f32[8,520,256]{2,1,0:T(8,128)}, f32[8,520,256]{2,1,0:T(8,128)}, f32[8,520,256]{2,1,0:T(8,128)}, f32[8,520,256]{2,1,0:T(8,128)}, f32[8,520,256]{2,1,0:T(8,128)}, /*index=5*/f32[8,520,256]{2,1,0:T(8,128)}) fusion(f32[10,520,258]{2,1,0:T(8,128)S(1)} %fusion.6), kind=kLoop, calls=%fused_computation.23 | loop fusion | flops 1064960 | bytes 54845440 | tf_op jit(solution)/shard_map/add | solution.py:131
  142.6 11.9 %fusion.8 = f32[8,512,256]{2,1,0:T(8,128)} fusion(f32[8,520,256]{2,1,0:T(8,128)} %get-tuple-element.6, s32[]{:T(128)S(6)} %select_n.94, f32[8,520,256]{2,1,0:T(8,128)} %get-tuple-element.7, f32[8,520,256]{2,1,0:T(8,128)} %get-tuple-element.8, f32[8,520,256]{2,1,0:T(8,128)} %get-tuple-element.10, f32[8,520,256]{2,1,0:T(8,128)} %get-tuple-element.9, ...), kind=kLoop, calls=%fused_computation.26 | loop fusion | flops 7340032 | bytes 29360132 | tf_op jit(solution)/shard_map/mul | solution.py:181
  154.5 4.6 %fusion.27 = (f32[8,256,256]{2,1,0:T(8,128)}, f32[8,256,256]{2,1,0:T(8,128)}) fusion(f32[8,512,256]{2,1,0:T(8,128)} %fusion.8), kind=kLoop, calls=%fused_computation.67 | loop fusion | bytes 8388608 | tf_op jit(solution)/shard_map/slice | solution.py:197
  159.1 5.4 %shard_map.82 = f32[2,256,256]{2,1,0:T(8,128)} custom-call(f32[2,8]{1,0:T(2,128)} %bitcast.31, f32[8,256,256]{2,1,0:T(8,128)} %get-tuple-element.15.refs_0_), custom_call_target="tpu_custom_call" | custom-call | flops 2097152 | bytes 2621440 | tf_op jit(solution)/shard_map/pallas_call | solution.py:116
  164.5 3.4 %collective-permute-start.5 = (f32[2,256,256]{2,1,0:T(8,128)}, f32[2,256,256]{2,1,0:T(8,128)S(1)}, u32[]{:S(2)}, u32[]{:S(2)}) collective-permute-start(f32[2,256,256]{2,1,0:T(8,128)} %shard_map.82), channel_id=1, source_target_pairs={{0,2},{1,3},{6,4},{7,5},{8,10},{9,11},{14,12},{15,13},{16,18},{17,... | collective-permute-start | bytes 1572872 | tf_op jit(solution)/shard_map/ppermute | solution.py:188
  167.9 5.4 %shard_map.86 = f32[2,256,256]{2,1,0:T(8,128)} custom-call(f32[2,8]{1,0:T(2,128)} %bitcast.32, f32[8,256,256]{2,1,0:T(8,128)} %get-tuple-element.16.refs_0_), custom_call_target="tpu_custom_call" | custom-call | flops 2097152 | bytes 2621440 | tf_op jit(solution)/shard_map/pallas_call | solution.py:116
  174.7 3.8 %collective-permute-done.5.refs_1_ = f32[2,256,256]{2,1,0:T(8,128)S(1)} collective-permute-done((f32[2,256,256]{2,1,0:T(8,128)}, f32[2,256,256]{2,1,0:T(8,128)S(1)}, u32[]{:S(2)}, u32[]{:S(2)}) %collective-permute-start.5) | collective-permute-done | bytes 524320 | tf_op jit(solution)/shard_map/ppermute | solution.py:188
  179.3 5.5 %shard_map.83 = f32[2,256,256]{2,1,0:T(8,128)} custom-call(f32[2,10]{1,0:T(2,128)} %fusion.23.matrix_ref, f32[8,256,256]{2,1,0:T(8,128)} %get-tuple-element.15.refs_0_, f32[2,256,256]{2,1,0:T(8,128)} %copy-done.5), custom_call_target="tpu_custom_call" | custom-call | flops 2621440 | bytes 3145728 | tf_op jit(solution)/shard_map/pallas_call | solution.py:116
  185.5 4.3 %collective-permute-done.9.refs_1_ = f32[2,256,256]{2,1,0:T(8,128)S(1)} collective-permute-done((f32[2,256,256]{2,1,0:T(8,128)}, f32[2,256,256]{2,1,0:T(8,128)S(1)}, u32[]{:S(2)}, u32[]{:S(2)}) %collective-permute-start.9) | collective-permute-done | bytes 524320 | tf_op jit(solution)/shard_map/ppermute | solution.py:188
  190.6 5.5 %shard_map.87 = f32[2,256,256]{2,1,0:T(8,128)} custom-call(f32[2,10]{1,0:T(2,128)} %fusion.23.matrix_ref, f32[8,256,256]{2,1,0:T(8,128)} %get-tuple-element.16.refs_0_, f32[2,256,256]{2,1,0:T(8,128)} %copy-done.4), custom_call_target="tpu_custom_call" | custom-call | flops 2621440 | bytes 3145728 | tf_op jit(solution)/shard_map/pallas_call | solution.py:116
  198.9 5.5 %shard_map.84 = f32[2,256,256]{2,1,0:T(8,128)} custom-call(f32[2,12]{1,0:T(2,128)} %fusion.24.matrix_ref, f32[8,256,256]{2,1,0:T(8,128)} %get-tuple-element.15.refs_0_, f32[2,256,256]{2,1,0:T(8,128)} %copy-done.5, f32[2,256,256]{2,1,0:T(8,128)} %copy-done.10), custom_call_target="tpu_custom_call" | custom-call | flops 3145728 | bytes 3670016 | tf_op jit(solution)/shard_map/pallas_call | solution.py:116
  206.5 5.5 %shard_map.88 = f32[2,256,256]{2,1,0:T(8,128)} custom-call(f32[2,12]{1,0:T(2,128)} %fusion.24.matrix_ref, f32[8,256,256]{2,1,0:T(8,128)} %get-tuple-element.16.refs_0_, f32[2,256,256]{2,1,0:T(8,128)} %copy-done.4, f32[2,256,256]{2,1,0:T(8,128)} %copy-done.8), custom_call_target="tpu_custom_call" | custom-call | flops 3145728 | bytes 3670016 | tf_op jit(solution)/shard_map/pallas_call | solution.py:116
  214.8 7.9 %collective-permute-done.7 = f32[2,256,256]{2,1,0:T(8,128)S(1)} collective-permute-done((f32[2,256,256]{2,1,0:T(8,128)}, f32[2,256,256]{2,1,0:T(8,128)S(1)}, u32[]{:S(2)}, u32[]{:S(2)}) %collective-permute-start.7) | collective-permute-done | bytes 524320 | tf_op jit(solution)/shard_map/ppermute | solution.py:188
  224.6 6.5 %shard_map.85 = f32[8,256,256]{2,1,0:T(8,128)} custom-call(f32[8,12]{1,0:T(8,128)} %dynamic-slice_bitcast_fusion.matrix_ref, f32[8,256,256]{2,1,0:T(8,128)} %get-tuple-element.15.refs_0_, f32[2,256,256]{2,1,0:T(8,128)} %copy-done.5, f32[2,256,256]{2,1,0:T(8,128)} %add.81.refs_2_), custom_call_target="tpu_custom_call" | custom-call | flops 12582912 | bytes 5242880 | tf_op jit(solution)/shard_map/pallas_call | solution.py:116
  235.4 6.6 %shard_map.89 = f32[8,256,256]{2,1,0:T(8,128)} custom-call(f32[8,12]{1,0:T(8,128)} %dynamic-slice_bitcast_fusion.matrix_ref, f32[8,256,256]{2,1,0:T(8,128)} %get-tuple-element.16.refs_0_, f32[2,256,256]{2,1,0:T(8,128)} %copy-done.4, f32[2,256,256]{2,1,0:T(8,128)} %add.82.refs_2_), custom_call_target="tpu_custom_call" | custom-call | flops 12582912 | bytes 5242880 | tf_op jit(solution)/shard_map/pallas_call | solution.py:116
  246.2 12.0 %collective-permute-done.8 = f32[4,256,256]{2,1,0:T(8,128)} collective-permute-done((f32[4,256,256]{2,1,0:T(8,128)S(1)}, f32[4,256,256]{2,1,0:T(8,128)}, u32[]{:S(2)}, u32[]{:S(2)}) %collective-permute-start.8) | collective-permute-done | bytes 1048608 | tf_op jit(solution)/shard_map/ppermute | solution.py:213
  259.7 21.0 %collective-permute-done.12 = f32[4,256,256]{2,1,0:T(8,128)} collective-permute-done((f32[4,256,256]{2,1,0:T(8,128)}, f32[4,256,256]{2,1,0:T(8,128)}, u32[]{:S(2)}, u32[]{:S(2)}) %collective-permute-start.12) | collective-permute-done | bytes 1048608 | tf_op jit(solution)/shard_map/ppermute | solution.py:213
  282.2 3.5 %fusion.11 = f32[4,4,1024]{2,0,1:T(4,128)S(1)} fusion(f32[4,256,1]{1,0,2:T(4,128)S(1)} %copy-done.11, f32[4,256,256]{2,1,0:T(8,128)S(1)} %get-tuple-element.20, f32[4,256,256]{2,1,0:T(8,128)S(1)} %get-tuple-element.18, f32[4,256,256]{2,1,0:T(8,128)S(1)} %get-tuple-element.19, f32[4,256,256]{2,1,0:T(8,128)S(1)} %get-tuple-element.17), kind=kOutput, calls=%fused_computation.36 | convolution fusion | flops 53477376 | bytes 4263936 | tf_op jit(solution)/shard_map/ij,axj->iax/dot_general | solution.py:218
  285.7 6.5 %all-gather = f32[4,4,4096]{2,1,0:T(4,128)} all-gather(f32[1,4,4096]{2,1,0:T(4,128)S(1)} %bitcast.30), channel_id=1, replica_groups=mesh['gy'=4,'gx'=8] {'gy'}, dimensions={0}, use_global_device_ids=true | all-gather | bytes 327680 | tf_op jit(solution)/shard_map/all_gather | solution.py:220
  293.4 5.5 %fusion.12 = f32[4,1024,256]{1,2,0:T(8,128)S(1)} fusion(f32[256,256,1]{1,0,2:T(8,128)} %constant.100, f32[4,256,256]{2,1,0:T(8,128)S(1)} %get-tuple-element.20, f32[4,256,256]{2,1,0:T(8,128)} %copy-done.6, f32[4,256,256]{2,1,0:T(8,128)S(1)} %get-tuple-element.19, f32[4,256,256]{2,1,0:T(8,128)S(1)} %get-tuple-element.17), kind=kOutput, calls=%fused_computation.37 | convolution fusion | flops 3224371200 | bytes 8650752 | tf_op jit(solution)/shard_map/axj,ji->axi/dot_general | solution.py:222
  299.0 6.0 %fusion.16 = f32[4,1024,256]{1,2,0:T(8,128)S(1)} fusion(f32[16,4,1024]{2,1,0:T(4,128)S(1)} %reshape.7, f32[4,256,16]{2,1,0:T(8,128)} %constant.93.clone, s32[]{:T(128)S(6)} %select_n.103), kind=kOutput, calls=%fused_computation.49 | convolution fusion | flops 201326592 | bytes 4587524 | tf_op jit(solution)/shard_map/qax,iq->axi/dot_general | solution.py:223
  305.0 15.1 %fusion.13 = f32[4,1024,256]{1,2,0:T(8,128)} fusion(f32[1024,1024,1]{1,0,2:T(8,128)S(1)} %copy-done.7, f32[4,1024,256]{1,2,0:T(8,128)S(1)} %fusion.12, f32[4,1024,256]{1,2,0:T(8,128)S(1)} %fusion.16), kind=kOutput, calls=%fused_computation.38 | convolution fusion | flops 12885950464 | bytes 16777216 | tf_op jit(solution)/shard_map/ij,ajb->aib/dot_general | solution.py:226
  320.1 5.4 %copy.14 = f32[4,1024,256]{2,1,0:T(8,128)} copy(f32[4,1024,256]{1,2,0:T(8,128)} %fusion.13) | data formatting | bytes 8388608 | tf_op jit(solution)/shard_map/ij,ajb->aib/transpose | solution.py:226
  (59 shorter events, 47.9 us)
Async XLA Ops:
  1.7 49.4 %collective-permute-start = (f32[4,520,256]{2,1,0:T(8,128)S(1)}, f32[4,520,256]{2,1,0:T(8,128)}, u32[]{:S(2)}, u32[]{:S(2)}) collective-permute-start(f32[4,520,256]{2,1,0:T(8,128)S(1)} %constant_dynamic-slice_fusion.2), channel_id=1, source_target_pairs={{0,1},{1,0},{2,3},{3,2},{4,5},{5,4},{6,7},{7,6},{8,9},{9,8},{10,11... | collective-permute-start | bytes 6389768 | tf_op jit(solution)/shard_map/ppermute | solution.py:159
  53.9 5.0 %copy-start.1 = (f32[4,520,256]{2,1,0:T(8,128)}, f32[4,520,256]{2,1,0:T(8,128)S(1)}, u32[]{:S(2)}) copy-start(f32[4,520,256]{2,1,0:T(8,128)S(1)} %get-tuple-element.14) | copy-start | bytes 6389764
  53.9 51.7 %copy-start = (f32[4,520,256]{2,1,0:T(8,128)}, f32[4,520,256]{2,1,0:T(8,128)S(1)}, u32[]{:S(2)}) copy-start(f32[4,520,256]{2,1,0:T(8,128)S(1)} %get-tuple-element.13) | copy-start | bytes 6389764
  55.1 25.9 %collective-permute-start.1 = (f32[2,520,256]{2,1,0:T(8,128)}, f32[2,520,256]{2,1,0:T(8,128)S(1)}, u32[]{:S(2)}, u32[]{:S(2)}) collective-permute-start(f32[2,520,256]{2,1,0:T(8,128)} %slice.118), channel_id=1, source_target_pairs={{0,2},{1,3},{2,4},{3,5},{4,6},{5,7},{8,10},{9,11},{10,12},{11,13},... | collective-permute-start | bytes 3194888 | tf_op jit(solution)/shard_map/ppermute | solution.py:161
  59.9 26.3 %collective-permute-start.2 = (f32[2,520,256]{2,1,0:T(8,128)}, f32[2,520,256]{2,1,0:T(8,128)}, u32[]{:S(2)}, u32[]{:S(2)}) collective-permute-start(f32[2,520,256]{2,1,0:T(8,128)} %slice.119), channel_id=1, source_target_pairs={{2,0},{3,1},{4,2},{5,3},{6,4},{7,5},{10,8},{11,9},{12,10},{13,11},... | collective-permute-start | bytes 3194888 | tf_op jit(solution)/shard_map/ppermute | solution.py:162
  94.6 5.4 %collective-permute-start.3 = (f32[2,12,520]{2,0,1:T(2,128)S(1)}, f32[2,12,520]{2,0,1:T(2,128)S(1)}, u32[]{:S(2)}, u32[]{:S(2)}) collective-permute-start(f32[2,12,520]{2,0,1:T(2,128)S(1)} %copy.10), channel_id=1, source_target_pairs={{0,8},{8,16},{16,24},{1,9},{9,17},{17,25},{2,10},{10,18},{18,26},{... | collective-permute-start | bytes 149768 | tf_op jit(solution)/shard_map/ppermute | solution.py:167
  98.5 4.9 %collective-permute-start.4 = (f32[2,12,520]{2,0,1:T(2,128)S(1)}, f32[2,12,520]{2,0,1:T(2,128)S(1)}, u32[]{:S(2)}, u32[]{:S(2)}) collective-permute-start(f32[2,12,520]{2,0,1:T(2,128)S(1)} %copy.12), channel_id=1, source_target_pairs={{8,0},{16,8},{24,16},{9,1},{17,9},{25,17},{10,2},{18,10},{26,18},{... | collective-permute-start | bytes 149768 | tf_op jit(solution)/shard_map/ppermute | solution.py:168
  164.5 14.0 %collective-permute-start.5 = (f32[2,256,256]{2,1,0:T(8,128)}, f32[2,256,256]{2,1,0:T(8,128)S(1)}, u32[]{:S(2)}, u32[]{:S(2)}) collective-permute-start(f32[2,256,256]{2,1,0:T(8,128)} %shard_map.82), channel_id=1, source_target_pairs={{0,2},{1,3},{6,4},{7,5},{8,10},{9,11},{14,12},{15,13},{16,18},{17,... | collective-permute-start | bytes 1572872 | tf_op jit(solution)/shard_map/ppermute | solution.py:188
  173.4 16.4 %collective-permute-start.9 = (f32[2,256,256]{2,1,0:T(8,128)}, f32[2,256,256]{2,1,0:T(8,128)S(1)}, u32[]{:S(2)}, u32[]{:S(2)}) collective-permute-start(f32[2,256,256]{2,1,0:T(8,128)} %shard_map.86), channel_id=1, source_target_pairs={{0,2},{1,3},{6,4},{7,5},{8,10},{9,11},{14,12},{15,13},{16,18},{17,... | collective-permute-start | bytes 1572872 | tf_op jit(solution)/shard_map/ppermute | solution.py:188
  178.5 0.8 copy-start.5
  184.8 13.3 %collective-permute-start.6 = (f32[2,256,256]{2,1,0:T(8,128)}, f32[2,256,256]{2,1,0:T(8,128)S(1)}, u32[]{:S(2)}, u32[]{:S(2)}) collective-permute-start(f32[2,256,256]{2,1,0:T(8,128)} %shard_map.83), channel_id=1, source_target_pairs={{2,4},{3,5},{4,2},{5,3},{10,12},{11,13},{12,10},{13,11},{18,20},{1... | collective-permute-start | bytes 1572872 | tf_op jit(solution)/shard_map/ppermute | solution.py:188
  189.8 0.8 copy-start.4
  196.1 9.6 %collective-permute-start.10 = (f32[2,256,256]{2,1,0:T(8,128)}, f32[2,256,256]{2,1,0:T(8,128)S(1)}, u32[]{:S(2)}, u32[]{:S(2)}) collective-permute-start(f32[2,256,256]{2,1,0:T(8,128)} %shard_map.87), channel_id=1, source_target_pairs={{2,4},{3,5},{4,2},{5,3},{10,12},{11,13},{12,10},{13,11},{18,20},{1... | collective-permute-start | bytes 1572872 | tf_op jit(solution)/shard_map/ppermute | solution.py:188
  198.0 0.8 copy-start.10
  204.4 18.3 %collective-permute-start.7 = (f32[2,256,256]{2,1,0:T(8,128)}, f32[2,256,256]{2,1,0:T(8,128)S(1)}, u32[]{:S(2)}, u32[]{:S(2)}) collective-permute-start(f32[2,256,256]{2,1,0:T(8,128)} %shard_map.84), channel_id=1, source_target_pairs={{2,0},{3,1},{4,6},{5,7},{10,8},{11,9},{12,14},{13,15},{18,16},{19,... | collective-permute-start | bytes 1572872 | tf_op jit(solution)/shard_map/ppermute | solution.py:188
  205.7 0.8 copy-start.8
  212.0 22.6 %collective-permute-start.11 = (f32[2,256,256]{2,1,0:T(8,128)}, f32[2,256,256]{2,1,0:T(8,128)S(1)}, u32[]{:S(2)}, u32[]{:S(2)}) collective-permute-start(f32[2,256,256]{2,1,0:T(8,128)} %shard_map.88), channel_id=1, source_target_pairs={{2,0},{3,1},{4,6},{5,7},{10,8},{11,9},{12,14},{13,15},{18,16},{19,... | collective-permute-start | bytes 1572872 | tf_op jit(solution)/shard_map/ppermute | solution.py:188
  224.6 10.0 %copy-start.9 = (f32[2,256,256]{2,1,0:T(8,128)S(1)}, f32[2,256,256]{2,1,0:T(8,128)}, u32[]{:S(2)}) copy-start(f32[2,256,256]{2,1,0:T(8,128)} %copy-done.8) | copy-start | bytes 1572868
  232.8 25.5 %collective-permute-start.8 = (f32[4,256,256]{2,1,0:T(8,128)S(1)}, f32[4,256,256]{2,1,0:T(8,128)}, u32[]{:S(2)}, u32[]{:S(2)}) collective-permute-start(f32[4,256,256]{2,1,0:T(8,128)S(1)} %slice_select_fusion.2), channel_id=1, source_target_pairs={{0,1},{1,0},{2,3},{3,2},{4,5},{5,4},{6,7},{7,6},{8,9},{9,8},{10,11... | collective-permute-start | bytes 3145736 | tf_op jit(solution)/shard_map/ppermute | solution.py:213
  235.4 22.8 %copy-start.2 = (f32[8,256,256]{2,1,0:T(8,128)S(1)}, f32[8,256,256]{2,1,0:T(8,128)}, u32[]{:S(2)}) copy-start(f32[8,256,256]{2,1,0:T(8,128)} %shard_map.85) | copy-start | bytes 6291460
  244.7 36.0 %collective-permute-start.12 = (f32[4,256,256]{2,1,0:T(8,128)}, f32[4,256,256]{2,1,0:T(8,128)}, u32[]{:S(2)}, u32[]{:S(2)}) collective-permute-start(f32[4,256,256]{2,1,0:T(8,128)} %slice_select_fusion), channel_id=1, source_target_pairs={{0,1},{1,0},{2,3},{3,2},{4,5},{5,4},{6,7},{7,6},{8,9},{9,8},{10,11... | collective-permute-start | bytes 3145736 | tf_op jit(solution)/shard_map/ppermute | solution.py:213
  246.2 34.5 %copy-start.3 = (f32[8,256,256]{2,1,0:T(8,128)S(1)}, f32[8,256,256]{2,1,0:T(8,128)}, u32[]{:S(2)}) copy-start(f32[8,256,256]{2,1,0:T(8,128)} %shard_map.89) | copy-start | bytes 6291460
  246.2 36.0 %copy-start.11 = (f32[4,256,1]{1,0,2:T(4,128)S(1)}, f32[4,256,1]{1,0,2:T(4,128)}, u32[]{:S(2)}) copy-start(f32[4,256,1]{1,0,2:T(4,128)} %constant.101) | copy-start | bytes 12292
  259.7 26.1 %copy-start.6 = (f32[4,256,256]{2,1,0:T(8,128)}, f32[4,256,256]{2,1,0:T(8,128)S(1)}, u32[]{:S(2)}) copy-start(f32[4,256,256]{2,1,0:T(8,128)S(1)} %get-tuple-element.18) | copy-start | bytes 3145732
  298.9 6.1 %copy-start.7 = (f32[1024,1024,1]{1,0,2:T(8,128)S(1)}, f32[1024,1024,1]{1,0,2:T(8,128)}, u32[]{:S(2)}) copy-start(f32[1024,1024,1]{1,0,2:T(8,128)} %constant.102) | copy-start | bytes 12582916

commit v2 on v1

--- a/solution.py
+++ b/solution.py
@@ -110,7 +110,7 @@
 def mix(matrix, *arrays):
     counts = tuple(a.shape[0] for a in arrays)
     rows, width = arrays[0].shape[1:]
-    tile = 32
+    tile = min(rows, 128)
     spec = lambda planes: pl.BlockSpec((planes, tile, width), lambda i: (0, i, 0))
     total = sum(counts) + matrix.shape[0]
     return pl.pallas_call(
@@ -127,19 +127,61 @@
     )(matrix, *arrays)
 
 
-def laplace_inner(padded):
-    total = padded[2:, 1:-1, 1:-1] + padded[:-2, 1:-1, 1:-1]
-    total = total + padded[1:-1, 2:, 1:-1] + padded[1:-1, :-2, 1:-1]
-    total = total + padded[1:-1, 1:-1, 2:] + padded[1:-1, 1:-1, :-2]
-    return total - 6.0 * padded[1:-1, 1:-1, 1:-1]
+def stencil_kernel(place_ref, wide_ref, out_ref, potential, whole):
+    planes, rows, width = wide_ref.shape
+    cells_y = out_ref.shape[2]
+    row = lax.broadcasted_iota(jnp.int32, (rows, width), 0)
+    column = lax.broadcasted_iota(jnp.int32, (rows, width), 1)
+
+    def laplace(ref, plane):
+        centre = ref[plane]
+        total = ref[plane - 1] + ref[plane + 1] - 6.0 * centre
+        total = total + jnp.where(row == 0, 0.0, pltpu.roll(centre, 1, 0))
+        total = total + jnp.where(row == rows - 1, 0.0, pltpu.roll(centre, rows - 1, 0))
+        return centre, total + pltpu.roll(centre, 1, 1) + pltpu.roll(centre, width - 1, 1)
+
+    @pl.loop(1, planes - 1)
+    def _(plane):
+        centre, around = laplace(wide_ref, plane)
+        value = centre * centre * centre - centre - around
+        hidden = (column == width - 1) & (place_ref[2] == 1)
+        hidden = hidden | ((column == cells_y) & (place_ref[3] == 1))
+        potential[plane - 1] = jnp.where(hidden, 0.0, value)
+
+    @pl.when(place_ref[0] == 1)
+    def _():
+        potential[0] = jnp.zeros((rows, width), jnp.float32)
+
+    @pl.when(place_ref[1] == 1)
+    def _():
+        potential[planes - 3] = jnp.zeros((rows, width), jnp.float32)
+
+    start = pl.multiple_of(place_ref[4] * 8, 8)
+
+    @pl.loop(1, planes - 3)
+    def _(plane):
+        whole[...] = STEP * laplace(potential, plane)[1]
+        out_ref[plane - 1] = whole[pl.ds(start, out_ref.shape[1]), :cells_y]
+
+
+def stencil(place, wide, cells_y):
+    planes, rows, width = wide.shape
+    vmem = pl.BlockSpec(memory_space=pltpu.VMEM)
+    return pl.pallas_call(
+        stencil_kernel,
+        in_specs=[pl.BlockSpec(memory_space=pltpu.SMEM), vmem],
+        out_specs=vmem,
+        out_shape=jax.ShapeDtypeStruct((planes - 4, rows - 8, cells_y), jnp.float32),
+        scratch_shapes=[
+            pltpu.VMEM((planes - 2, rows, width), jnp.float32),
+            pltpu.VMEM((rows, width), jnp.float32),
+        ],
+        compiler_params=pltpu.CompilerParams(vmem_limit_bytes=44 * 2**20),
+    )(place, wide)
 
 
 def pick(table, index):
     return lax.dynamic_index_in_dim(jnp.asarray(table), index, 0, keepdims=False)
-
-
-def pad_x(values):
-    return jnp.pad(values, ((0, 0), (1, 1), (0, 0)))
 
 
 def body(concentration):
@@ -166,20 +208,12 @@
     columns = lambda v: jnp.moveaxis(v, 2, 0)
     before = lax.ppermute(columns(block[:, :, -HALO:]), "gy", right)
     behind = lax.ppermute(columns(block[:, :, :HALO]), "gy", left)
+    filler = jnp.zeros(block.shape[:2] + (128 - 2 * HALO,), jnp.float32)
     wide = jnp.concatenate(
-        [jnp.moveaxis(before, 0, 2), block, jnp.moveaxis(behind, 0, 2)], axis=2
+        [block, jnp.moveaxis(behind, 0, 2), filler, jnp.moveaxis(before, 0, 2)], axis=2
     )
-    centre = wide[1:-1, :, 1:-1]
-    potential = centre * centre * centre - centre - laplace_inner(pad_x(wide))
-    layer = lax.broadcasted_iota(jnp.int32, potential.shape, 0)
-    column = lax.broadcasted_iota(jnp.int32, potential.shape, 2)
-    outside = (layer == 0) & (group == 0)
-    outside |= (layer == potential.shape[0] - 1) & (group == groups - 1)
-    outside |= (column == 0) & (rank_y == 0)
-    outside |= (column == cells_y + 1) & (rank_y == blocks - 1)
-    potential = jnp.where(outside, 0.0, potential)
-    source = STEP * laplace_inner(pad_x(potential))
-    source = lax.dynamic_slice_in_dim(source, side * 8, half_x, 1)
+    place = [group == 0, group == groups - 1, rank_y == 0, rank_y == blocks - 1, side == 1]
+    source = stencil(jnp.stack(place).astype(jnp.int32), wide, cells_y)
 
     edge_map, out_map, full_map = two_ended_maps(planes * count, groups)
     edge_map, out_map, full_map = (pick(t, group) for t in (edge_map, out_map, full_map))

time: 327 us -> 291 us (0.89)
  other arithmetic: 63.8 us -> 24 us
  waiting for transfers between devices: 121 us -> 133 us
  Pallas kernels: 45.9 us -> 38.5 us
    pallas_call x8, Pallas kernels: 45.9 us -> 23.6 us  [mix(): pl.pallas_call(functools.partial(mix_kernel, counts), grid=(rows // tile,...]
    select_n x1 -> x0, other arithmetic: 17.2 us -> none  [body(): potential = jnp.where(outside, 0.0, potential)]
    pallas_call x0 -> x1, Pallas kernels: none -> 14.9 us  [stencil(): pl.pallas_call(stencil_kernel, in_specs=[pl.BlockSpec(memory_space=pltpu....]
    ppermute x6, waiting for transfers between devices: 16.2 us -> 29 us  [hop(): lax.ppermute(values, 'gx', [(2 * a + s, 2 * b + s) for a, b in sends for...]
    mul x1 -> x0, other arithmetic: 11.9 us -> none  [body(): source = STEP * laplace_inner(pad_x(potential))]
    add x1 -> x0, other arithmetic: 11.5 us -> none  [laplace_inner(): total = padded[2:, 1:-1, 1:-1] + padded[:-2, 1:-1, 1:-1]]
  transfers between devices with their start and end apart: 13 -> 13, of which waited for: 10 -> 9; matrix products, arithmetic and copies ran while one was open for 6% -> 6% of each run, Pallas kernels for 12% -> 7%
where the time goes in v2:
time: 291 us; the launch traced here: 290 us
  waiting for transfers between devices  133 us (46%)
  Pallas kernels  38.5 us (13%)
  local copies, waits for them, and re-layouts  33.5 us (12%)
  matrix products  30.1 us (10%)
  starting transfers between devices  24.2 us (8%)
  other arithmetic  24 us (8%)
  blocking collectives  6.46 us (2%)
    ppermute x1, waiting for transfers between devices, body(): got = lax.ppermute(give, 'gx', partner)  46.4 us
    ppermute x2, waiting for transfers between devices, body(): back = lax.ppermute(send, 'gx', partner)  32.5 us
    ppermute x6, waiting for transfers between devices, hop(): lax.ppermute(values, 'gx', [(2 * a + s, 2 * b + s) for a, b in sends for...  29 us
    pallas_call x8, Pallas kernels, mix(): pl.pallas_call(functools.partial(mix_kernel, counts), grid=(rows // tile,...  23.6 us
    ppermute x1, waiting for transfers between devices, body(): below = lax.ppermute(high[-HALO:], 'gx', up)  19.8 us
    dot_general x1, matrix products, body(): return jnp.einsum('ij,ajb->aib', inverse_x, after_y, precision=FINE)  15.1 us
    pallas_call x1, Pallas kernels, stencil(): pl.pallas_call(stencil_kernel, in_specs=[pl.BlockSpec(memory_space=pltpu....  14.9 us
    concatenate x1, other arithmetic, body(): jnp.concatenate([block, jnp.moveaxis(behind, 0, 2), filler, jnp.moveaxis(...  9.07 us
  transfers between devices with their start and end apart: 13, of which 9 were waited for; matrix products, arithmetic and copies ran while one was open for 6% of the time, Pallas kernels for 7%

profile of v2, /device:TPU:0, one launch (start us, length us, event | category | flops | bytes accessed | tf_op | source)
XLA Modules:
  0.0 290.1 jit_solution(13413260271457945250)
XLA Ops:
  1.7 3.0 %collective-permute-start = (f32[4,520,256]{2,1,0:T(8,128)S(1)}, f32[4,520,256]{2,1,0:T(8,128)}, u32[]{:S(2)}, u32[]{:S(2)}) collective-permute-start(f32[4,520,256]{2,1,0:T(8,128)S(1)} %constant_dynamic-slice_fusion.2), channel_id=1, source_target_pairs={{0,1},{1,0},{2,3},{3,2},{4,5},{5,4},{6,7},{7,6},{8,9},{9,8},{10,11... | collective-permute-start | bytes 6389768 | tf_op jit(solution)/shard_map/ppermute | solution.py:201
  4.7 46.4 %collective-permute-done = f32[4,520,256]{2,1,0:T(8,128)} collective-permute-done((f32[4,520,256]{2,1,0:T(8,128)S(1)}, f32[4,520,256]{2,1,0:T(8,128)}, u32[]{:S(2)}, u32[]{:S(2)}) %collective-permute-start) | collective-permute-done | bytes 2129952 | tf_op jit(solution)/shard_map/ppermute | solution.py:201
  51.2 2.7 dynamic-slice_select_fusion.1
  55.1 3.8 %collective-permute-start.1 = (f32[2,520,256]{2,1,0:T(8,128)}, f32[2,520,256]{2,1,0:T(8,128)S(1)}, u32[]{:S(2)}, u32[]{:S(2)}) collective-permute-start(f32[2,520,256]{2,1,0:T(8,128)} %slice.49), channel_id=1, source_target_pairs={{0,2},{1,3},{2,4},{3,5},{4,6},{5,7},{8,10},{9,11},{10,12},{11,13},... | collective-permute-start | bytes 3194888 | tf_op jit(solution)/shard_map/ppermute | solution.py:203
  61.2 19.8 %collective-permute-done.1 = f32[2,520,256]{2,1,0:T(8,128)S(1)} collective-permute-done((f32[2,520,256]{2,1,0:T(8,128)}, f32[2,520,256]{2,1,0:T(8,128)S(1)}, u32[]{:S(2)}, u32[]{:S(2)}) %collective-permute-start.1) | collective-permute-done | bytes 1064992 | tf_op jit(solution)/shard_map/ppermute | solution.py:203
  81.0 5.2 %collective-permute-done.2 = f32[2,520,256]{2,1,0:T(8,128)} collective-permute-done((f32[2,520,256]{2,1,0:T(8,128)}, f32[2,520,256]{2,1,0:T(8,128)}, u32[]{:S(2)}, u32[]{:S(2)}) %collective-permute-start.2) | collective-permute-done | bytes 1064992 | tf_op jit(solution)/shard_map/ppermute | solution.py:204
  88.4 3.7 %slice_bitcast_fusion.1 = (f32[2,12,520]{0,2,1:T(8,128)}, f32[2,12,520]{0,2,1:T(8,128)}) fusion(f32[12,520,256]{2,1,0:T(8,128)S(1)} %pad_maximum_fusion.1), kind=kLoop, calls=%fused_computation.6 | loop fusion | bytes 199680 | tf_op jit(solution)/shard_map/transpose | solution.py:208
  92.1 2.6 copy.10
  96.0 2.6 copy.12
  98.5 3.0 %collective-permute-start.4 = (f32[2,12,520]{2,0,1:T(2,128)S(1)}, f32[2,12,520]{2,0,1:T(2,128)S(1)}, u32[]{:S(2)}, u32[]{:S(2)}) collective-permute-start(f32[2,12,520]{2,0,1:T(2,128)S(1)} %copy.12), channel_id=1, source_target_pairs={{0,8},{8,16},{16,24},{1,9},{9,17},{17,25},{2,10},{10,18},{18,26},{... | collective-permute-start | bytes 149768 | tf_op jit(solution)/shard_map/ppermute | solution.py:209
  107.5 9.1 %pad_maximum_fusion.wide_ref = f32[12,520,384]{2,1,0:T(8,128)} fusion(f32[12,520,2]{2,1,0:T(8,128)} %bitcast.32, f32[12,520,2]{2,1,0:T(8,128)} %bitcast.31, f32[2,520,256]{2,1,0:T(8,128)} %collective-permute-done.2, f32[4,520,256]{2,1,0:T(8,128)S(1)} %get-tuple-element.7, f32[4,520,256]{2,1,0:T(8,128)} %copy-done, ...), kind=kLoop, calls=%fused_computation | loop fusion | flops 14376960 | bytes 16075776 | tf_op jit(solution)/shard_map/concatenate | solution.py:212
  116.6 14.9 %shard_map.82 = f32[8,512,256]{2,1,0:T(8,128)S(1)} custom-call(s32[5]{0:T(128)S(1)} %convert_element_type.3.place_ref, f32[12,520,384]{2,1,0:T(8,128)} %pad_maximum_fusion.wide_ref), custom_call_target="tpu_custom_call" | custom-call | tf_op jit(solution)/shard_map/pallas_call | solution.py:170
  136.3 3.4 %collective-permute-start.5 = (f32[2,256,256]{2,1,0:T(8,128)}, f32[2,256,256]{2,1,0:T(8,128)S(1)}, u32[]{:S(2)}, u32[]{:S(2)}) collective-permute-start(f32[2,256,256]{2,1,0:T(8,128)} %shard_map.83), channel_id=1, source_target_pairs={{0,2},{1,3},{6,4},{7,5},{8,10},{9,11},{14,12},{15,13},{16,18},{17,... | collective-permute-start | bytes 1572872 | tf_op jit(solution)/shard_map/ppermute | solution.py:222
  139.7 2.4 shard_map.87
  143.5 8.7 %collective-permute-done.5.refs_1_ = f32[2,256,256]{2,1,0:T(8,128)S(1)} collective-permute-done((f32[2,256,256]{2,1,0:T(8,128)}, f32[2,256,256]{2,1,0:T(8,128)S(1)}, u32[]{:S(2)}, u32[]{:S(2)}) %collective-permute-start.5) | collective-permute-done | bytes 524320 | tf_op jit(solution)/shard_map/ppermute | solution.py:222
  153.0 2.6 shard_map.84
  156.2 7.2 %collective-permute-done.9.refs_1_ = f32[2,256,256]{2,1,0:T(8,128)S(1)} collective-permute-done((f32[2,256,256]{2,1,0:T(8,128)}, f32[2,256,256]{2,1,0:T(8,128)S(1)}, u32[]{:S(2)}, u32[]{:S(2)}) %collective-permute-start.9) | collective-permute-done | bytes 524320 | tf_op jit(solution)/shard_map/ppermute | solution.py:222
  164.2 2.6 shard_map.88
  169.5 2.7 shard_map.85
  174.4 2.8 shard_map.89
  179.9 11.2 %collective-permute-done.7 = f32[2,256,256]{2,1,0:T(8,128)S(1)} collective-permute-done((f32[2,256,256]{2,1,0:T(8,128)}, f32[2,256,256]{2,1,0:T(8,128)S(1)}, u32[]{:S(2)}, u32[]{:S(2)}) %collective-permute-start.7) | collective-permute-done | bytes 524320 | tf_op jit(solution)/shard_map/ppermute | solution.py:222
  192.9 4.0 %shard_map.86 = f32[8,256,256]{2,1,0:T(8,128)} custom-call(f32[8,12]{1,0:T(8,128)} %dynamic-slice_bitcast_fusion.matrix_ref, f32[8,256,256]{2,1,0:T(8,128)} %get-tuple-element.9.refs_0_, f32[2,256,256]{2,1,0:T(8,128)} %copy-done.4, f32[2,256,256]{2,1,0:T(8,128)} %add.33.refs_2_), custom_call_target="tpu_custom_call" | custom-call | flops 12582912 | bytes 5242880 | tf_op jit(solution)/shard_map/pallas_call | solution.py:116
  203.2 4.1 %shard_map.90 = f32[8,256,256]{2,1,0:T(8,128)} custom-call(f32[8,12]{1,0:T(8,128)} %dynamic-slice_bitcast_fusion.matrix_ref, f32[8,256,256]{2,1,0:T(8,128)} %get-tuple-element.10.refs_0_, f32[2,256,256]{2,1,0:T(8,128)} %copy-done.3, f32[2,256,256]{2,1,0:T(8,128)} %add.34.refs_2_), custom_call_target="tpu_custom_call" | custom-call | flops 12582912 | bytes 5242880 | tf_op jit(solution)/shard_map/pallas_call | solution.py:116
  207.3 2.7 slice_select_fusion
  211.5 13.5 %collective-permute-done.8 = f32[4,256,256]{2,1,0:T(8,128)} collective-permute-done((f32[4,256,256]{2,1,0:T(8,128)S(1)}, f32[4,256,256]{2,1,0:T(8,128)}, u32[]{:S(2)}, u32[]{:S(2)}) %collective-permute-start.8) | collective-permute-done | bytes 1048608 | tf_op jit(solution)/shard_map/ppermute | solution.py:247
  226.4 19.0 %collective-permute-done.12 = f32[4,256,256]{2,1,0:T(8,128)} collective-permute-done((f32[4,256,256]{2,1,0:T(8,128)}, f32[4,256,256]{2,1,0:T(8,128)}, u32[]{:S(2)}, u32[]{:S(2)}) %collective-permute-start.12) | collective-permute-done | bytes 1048608 | tf_op jit(solution)/shard_map/ppermute | solution.py:247
  246.9 3.5 %fusion.2 = f32[4,4,1024]{2,0,1:T(4,128)S(1)} fusion(f32[4,256,1]{1,0,2:T(4,128)S(1)} %copy-done.10, f32[4,256,256]{2,1,0:T(8,128)S(1)} %get-tuple-element.14, f32[4,256,256]{2,1,0:T(8,128)S(1)} %get-tuple-element.12, f32[4,256,256]{2,1,0:T(8,128)S(1)} %get-tuple-element.13, f32[4,256,256]{2,1,0:T(8,128)S(1)} %get-tuple-element.11), kind=kOutput, calls=%fused_computation.7 | convolution fusion | flops 53477376 | bytes 4263936 | tf_op jit(solution)/shard_map/ij,axj->iax/dot_general | solution.py:252
  250.4 6.5 %all-gather = f32[4,4,4096]{2,1,0:T(4,128)} all-gather(f32[1,4,4096]{2,1,0:T(4,128)S(1)} %bitcast.33), channel_id=1, replica_groups=mesh['gy'=4,'gx'=8] {'gy'}, dimensions={0}, use_global_device_ids=true | all-gather | bytes 327680 | tf_op jit(solution)/shard_map/all_gather | solution.py:254
  258.0 5.5 %fusion.3 = f32[4,1024,256]{1,2,0:T(8,128)S(1)} fusion(f32[256,256,1]{1,0,2:T(8,128)} %constant.81, f32[4,256,256]{2,1,0:T(8,128)S(1)} %get-tuple-element.14, f32[4,256,256]{2,1,0:T(8,128)} %copy-done.5, f32[4,256,256]{2,1,0:T(8,128)S(1)} %get-tuple-element.13, f32[4,256,256]{2,1,0:T(8,128)S(1)} %get-tuple-element.11), kind=kOutput, calls=%fused_computation.8 | convolution fusion | flops 3224371200 | bytes 8650752 | tf_op jit(solution)/shard_map/axj,ji->axi/dot_general | solution.py:256
  263.5 6.0 %fusion.7 = f32[4,1024,256]{1,2,0:T(8,128)S(1)} fusion(f32[16,4,1024]{2,1,0:T(4,128)S(1)} %reshape.7, f32[4,256,16]{2,1,0:T(8,128)} %constant.78.clone, s32[]{:T(128)S(6)} %select_n.94), kind=kOutput, calls=%fused_computation.20 | convolution fusion | flops 201326592 | bytes 4587524 | tf_op jit(solution)/shard_map/qax,iq->axi/dot_general | solution.py:257
  269.6 15.1 %fusion.4 = f32[4,1024,256]{1,2,0:T(8,128)} fusion(f32[1024,1024,1]{1,0,2:T(8,128)S(1)} %copy-done.6, f32[4,1024,256]{1,2,0:T(8,128)S(1)} %fusion.3, f32[4,1024,256]{1,2,0:T(8,128)S(1)} %fusion.7), kind=kOutput, calls=%fused_computation.9 | convolution fusion | flops 12885950464 | bytes 16777216 | tf_op jit(solution)/shard_map/ij,ajb->aib/dot_general | solution.py:260
  284.7 5.4 %copy.14 = f32[4,1024,256]{2,1,0:T(8,128)} copy(f32[4,1024,256]{1,2,0:T(8,128)} %fusion.4) | data formatting | bytes 8388608 | tf_op jit(solution)/shard_map/ij,ajb->aib/transpose | solution.py:260
  (57 shorter events, 44.3 us)
Async XLA Ops:
  1.7 49.4 %collective-permute-start = (f32[4,520,256]{2,1,0:T(8,128)S(1)}, f32[4,520,256]{2,1,0:T(8,128)}, u32[]{:S(2)}, u32[]{:S(2)}) collective-permute-start(f32[4,520,256]{2,1,0:T(8,128)S(1)} %constant_dynamic-slice_fusion.2), channel_id=1, source_target_pairs={{0,1},{1,0},{2,3},{3,2},{4,5},{5,4},{6,7},{7,6},{8,9},{9,8},{10,11... | collective-permute-start | bytes 6389768 | tf_op jit(solution)/shard_map/ppermute | solution.py:201
  53.9 5.0 %copy-start = (f32[4,520,256]{2,1,0:T(8,128)}, f32[4,520,256]{2,1,0:T(8,128)S(1)}, u32[]{:S(2)}) copy-start(f32[4,520,256]{2,1,0:T(8,128)S(1)} %get-tuple-element.8) | copy-start | bytes 6389764
  55.1 25.9 %collective-permute-start.1 = (f32[2,520,256]{2,1,0:T(8,128)}, f32[2,520,256]{2,1,0:T(8,128)S(1)}, u32[]{:S(2)}, u32[]{:S(2)}) collective-permute-start(f32[2,520,256]{2,1,0:T(8,128)} %slice.49), channel_id=1, source_target_pairs={{0,2},{1,3},{2,4},{3,5},{4,6},{5,7},{8,10},{9,11},{10,12},{11,13},... | collective-permute-start | bytes 3194888 | tf_op jit(solution)/shard_map/ppermute | solution.py:203
  59.9 26.3 %collective-permute-start.2 = (f32[2,520,256]{2,1,0:T(8,128)}, f32[2,520,256]{2,1,0:T(8,128)}, u32[]{:S(2)}, u32[]{:S(2)}) collective-permute-start(f32[2,520,256]{2,1,0:T(8,128)} %slice.50), channel_id=1, source_target_pairs={{2,0},{3,1},{4,2},{5,3},{6,4},{7,5},{10,8},{11,9},{12,10},{13,11},... | collective-permute-start | bytes 3194888 | tf_op jit(solution)/shard_map/ppermute | solution.py:204
  94.7 8.3 %collective-permute-start.3 = (f32[2,12,520]{2,0,1:T(2,128)S(1)}, f32[2,12,520]{2,0,1:T(2,128)S(1)}, u32[]{:S(2)}, u32[]{:S(2)}) collective-permute-start(f32[2,12,520]{2,0,1:T(2,128)S(1)} %copy.10), channel_id=1, source_target_pairs={{8,0},{16,8},{24,16},{9,1},{17,9},{25,17},{10,2},{18,10},{26,18},{... | collective-permute-start | bytes 149768 | tf_op jit(solution)/shard_map/ppermute | solution.py:210
  98.5 6.8 %collective-permute-start.4 = (f32[2,12,520]{2,0,1:T(2,128)S(1)}, f32[2,12,520]{2,0,1:T(2,128)S(1)}, u32[]{:S(2)}, u32[]{:S(2)}) collective-permute-start(f32[2,12,520]{2,0,1:T(2,128)S(1)} %copy.12), channel_id=1, source_target_pairs={{0,8},{8,16},{16,24},{1,9},{9,17},{17,25},{2,10},{10,18},{18,26},{... | collective-permute-start | bytes 149768 | tf_op jit(solution)/shard_map/ppermute | solution.py:209
  136.3 15.8 %collective-permute-start.5 = (f32[2,256,256]{2,1,0:T(8,128)}, f32[2,256,256]{2,1,0:T(8,128)S(1)}, u32[]{:S(2)}, u32[]{:S(2)}) collective-permute-start(f32[2,256,256]{2,1,0:T(8,128)} %shard_map.83), channel_id=1, source_target_pairs={{0,2},{1,3},{6,4},{7,5},{8,10},{9,11},{14,12},{15,13},{16,18},{17,... | collective-permute-start | bytes 1572872 | tf_op jit(solution)/shard_map/ppermute | solution.py:222
  142.2 21.2 %collective-permute-start.9 = (f32[2,256,256]{2,1,0:T(8,128)}, f32[2,256,256]{2,1,0:T(8,128)S(1)}, u32[]{:S(2)}, u32[]{:S(2)}) collective-permute-start(f32[2,256,256]{2,1,0:T(8,128)} %shard_map.87), channel_id=1, source_target_pairs={{0,2},{1,3},{6,4},{7,5},{8,10},{9,11},{14,12},{15,13},{16,18},{17,... | collective-permute-start | bytes 1572872 | tf_op jit(solution)/shard_map/ppermute | solution.py:222
  152.1 0.8 copy-start.4
  155.5 13.2 %collective-permute-start.6 = (f32[2,256,256]{2,1,0:T(8,128)}, f32[2,256,256]{2,1,0:T(8,128)S(1)}, u32[]{:S(2)}, u32[]{:S(2)}) collective-permute-start(f32[2,256,256]{2,1,0:T(8,128)} %shard_map.84), channel_id=1, source_target_pairs={{2,4},{3,5},{4,2},{5,3},{10,12},{11,13},{12,10},{13,11},{18,20},{1... | collective-permute-start | bytes 1572872 | tf_op jit(solution)/shard_map/ppermute | solution.py:222
  163.4 0.8 copy-start.3
  166.8 6.8 %collective-permute-start.10 = (f32[2,256,256]{2,1,0:T(8,128)}, f32[2,256,256]{2,1,0:T(8,128)S(1)}, u32[]{:S(2)}, u32[]{:S(2)}) collective-permute-start(f32[2,256,256]{2,1,0:T(8,128)} %shard_map.88), channel_id=1, source_target_pairs={{2,4},{3,5},{4,2},{5,3},{10,12},{11,13},{12,10},{13,11},{18,20},{1... | collective-permute-start | bytes 1572872 | tf_op jit(solution)/shard_map/ppermute | solution.py:222
  168.7 0.8 copy-start.9
  172.3 18.8 %collective-permute-start.7 = (f32[2,256,256]{2,1,0:T(8,128)}, f32[2,256,256]{2,1,0:T(8,128)S(1)}, u32[]{:S(2)}, u32[]{:S(2)}) collective-permute-start(f32[2,256,256]{2,1,0:T(8,128)} %shard_map.85), channel_id=1, source_target_pairs={{2,0},{3,1},{4,6},{5,7},{10,8},{11,9},{12,14},{13,15},{18,16},{19,... | collective-permute-start | bytes 1572872 | tf_op jit(solution)/shard_map/ppermute | solution.py:222
  173.5 0.8 copy-start.7
  177.1 25.1 %collective-permute-start.11 = (f32[2,256,256]{2,1,0:T(8,128)}, f32[2,256,256]{2,1,0:T(8,128)S(1)}, u32[]{:S(2)}, u32[]{:S(2)}) collective-permute-start(f32[2,256,256]{2,1,0:T(8,128)} %shard_map.89), channel_id=1, source_target_pairs={{2,0},{3,1},{4,6},{5,7},{10,8},{11,9},{12,14},{13,15},{18,16},{19,... | collective-permute-start | bytes 1572872 | tf_op jit(solution)/shard_map/ppermute | solution.py:222
  192.9 9.3 %copy-start.8 = (f32[2,256,256]{2,1,0:T(8,128)S(1)}, f32[2,256,256]{2,1,0:T(8,128)}, u32[]{:S(2)}) copy-start(f32[2,256,256]{2,1,0:T(8,128)} %copy-done.7) | copy-start | bytes 1572868
  198.7 26.3 %collective-permute-start.8 = (f32[4,256,256]{2,1,0:T(8,128)S(1)}, f32[4,256,256]{2,1,0:T(8,128)}, u32[]{:S(2)}, u32[]{:S(2)}) collective-permute-start(f32[4,256,256]{2,1,0:T(8,128)S(1)} %slice_select_fusion.2), channel_id=1, source_target_pairs={{0,1},{1,0},{2,3},{3,2},{4,5},{5,4},{6,7},{7,6},{8,9},{9,8},{10,11... | collective-permute-start | bytes 3145736 | tf_op jit(solution)/shard_map/ppermute | solution.py:247
  203.2 21.8 %copy-start.1 = (f32[8,256,256]{2,1,0:T(8,128)S(1)}, f32[8,256,256]{2,1,0:T(8,128)}, u32[]{:S(2)}) copy-start(f32[8,256,256]{2,1,0:T(8,128)} %shard_map.86) | copy-start | bytes 6291460
  210.0 35.4 %collective-permute-start.12 = (f32[4,256,256]{2,1,0:T(8,128)}, f32[4,256,256]{2,1,0:T(8,128)}, u32[]{:S(2)}, u32[]{:S(2)}) collective-permute-start(f32[4,256,256]{2,1,0:T(8,128)} %slice_select_fusion), channel_id=1, source_target_pairs={{0,1},{1,0},{2,3},{3,2},{4,5},{5,4},{6,7},{7,6},{8,9},{9,8},{10,11... | collective-permute-start | bytes 3145736 | tf_op jit(solution)/shard_map/ppermute | solution.py:247
  211.4 33.9 %copy-start.2 = (f32[8,256,256]{2,1,0:T(8,128)S(1)}, f32[8,256,256]{2,1,0:T(8,128)}, u32[]{:S(2)}) copy-start(f32[8,256,256]{2,1,0:T(8,128)} %shard_map.90) | copy-start | bytes 6291460
  211.4 35.4 %copy-start.10 = (f32[4,256,1]{1,0,2:T(4,128)S(1)}, f32[4,256,1]{1,0,2:T(4,128)}, u32[]{:S(2)}) copy-start(f32[4,256,1]{1,0,2:T(4,128)} %constant.82) | copy-start | bytes 12292
  226.4 24.0 %copy-start.5 = (f32[4,256,256]{2,1,0:T(8,128)}, f32[4,256,256]{2,1,0:T(8,128)S(1)}, u32[]{:S(2)}) copy-start(f32[4,256,256]{2,1,0:T(8,128)S(1)} %get-tuple-element.12) | copy-start | bytes 3145732
  263.5 6.1 %copy-start.6 = (f32[1024,1024,1]{1,0,2:T(8,128)S(1)}, f32[1024,1024,1]{1,0,2:T(8,128)}, u32[]{:S(2)}) copy-start(f32[1024,1024,1]{1,0,2:T(8,128)} %constant.83) | copy-start | bytes 12582916
